TPU v7x, 128 devices: a whole 4x4x4 slice. The times are simulated.
128 devices in a mesh: grp: 8 (over x, z_hi), row: 4 (over z_lo, core), col: 4 (over y).
Axes of the slice: x: 4, y: 4, z: 4 (z_hi: 2, z_lo: 2; z = z_hi * 2 + z_lo), core: 2. Of those that a mesh axis runs over, the one named last changes fastest.
Arguments:
- children: float32 [8, 6144, 6144], P('grp', 'row', 'col'), may hold values from -4 to 4
- child_map: int32 [8, 48], replicated, may hold values from 0 to 95, as said below
- panel_inverse: float32 [1024, 1024], P('row'), may hold values from -0.03125 to 0.03125
- pattern: int32 [88, 88], replicated, may hold values 0 or 1
Outputs:
- front: float32 [12288, 12288], P('row', ('grp', 'col'))
- panel_rows: float32 [1024, 12288], P('row', ('grp', 'col'))
Inputs may be any that keep to these rules, and one draw needn't show every extreme that they name: Each row of child_map is strictly increasing, and child tile a lies in parent tile block a // 12: child_map[g, a] // 24 == a // 12. In each row of child_map and each block, at most 2 child tiles land in any one run of 3 parent tiles that starts at a multiple of 3, and some run receives exactly 2.
All inputs are finite; a program needn't handle non-finite values.
Results may differ from a plain program's by a relative error of at most 0.000071.
Values sent between devices are 32-bit elements; how exact they have to be, the bound alone decides.
A program may use at most 128 MiB of HBM per device.

v0:
```python
import jax
import jax.numpy as jnp
from jax import lax
from jax.sharding import PartitionSpec as P

B = 128
PT = 96
WT = 8
W = 1024


def broadcast(value, axis, source):
    kept = jnp.where(lax.axis_index(axis) == source, value, 0).astype(value.dtype)
    return lax.psum(kept, axis)


def per_device(children, child_map, panel_inverse, pattern):
    member = lax.axis_index("grp")
    row_index = lax.axis_index("row")
    col_index = lax.axis_index("col")
    groups = lax.axis_size("grp")
    row_count = lax.axis_size("row")
    block = children[0]
    child_tiles = block.shape[0] // B
    parent_tiles = PT // row_count
    share = PT // (lax.axis_size("col") * groups)
    all_cols = (
        lax.dynamic_slice_in_dim(child_map, col_index * child_tiles, child_tiles, 1)
        - col_index * parent_tiles
    )
    col_map = lax.dynamic_index_in_dim(all_cols, member, 0, keepdims=False)
    strips = block.reshape(child_tiles * B, child_tiles, B)
    row_maps = (
        lax.dynamic_slice_in_dim(child_map, row_index * child_tiles, child_tiles, 1)
        - row_index * parent_tiles
    )
    row_select = (
        row_maps[:, None, :] == jnp.arange(parent_tiles, dtype=jnp.int32)[None, :, None]
    ).astype(jnp.float32)
    targets = jnp.arange(parent_tiles, dtype=jnp.int32).reshape(groups, share)
    col_select = (col_map[None, None, :] == targets[:, :, None]).astype(jnp.float32)
    spread = jnp.einsum("gsq,iqb->gisb", col_select, strips, precision=lax.Precision.HIGHEST)
    spread = spread.reshape(groups, child_tiles * B, share * B)
    received = lax.all_to_all(spread, "grp", split_axis=0, concat_axis=0, tiled=True)
    width = received.shape[2]
    pieces = received.reshape(groups, child_tiles, B, width)
    placed = jnp.einsum("smq,sqbn->mbn", row_select, pieces, precision=lax.Precision.HIGHEST)
    assembled = placed.reshape(parent_tiles * B, width)
    top = broadcast(assembled[:W], "row", 0)
    factor_part = jnp.dot(panel_inverse, top, precision=lax.Precision.HIGHEST)
    factor_own = lax.all_gather(factor_part, "row", axis=0, tiled=True)
    factor_peer = broadcast(factor_own, "col", row_index)
    tile_mask = jnp.zeros((PT, PT), jnp.float32).at[WT:, WT:].set(pattern.astype(jnp.float32))
    local_mask = lax.dynamic_slice(
        tile_mask,
        (row_index * parent_tiles, col_index * parent_tiles + member * share),
        (parent_tiles, share),
    )
    weights = jnp.broadcast_to(local_mask[:, None, :, None], (parent_tiles, B, share, B)).reshape(
        parent_tiles * B, share * B
    )
    product = lax.dot_general(
        lax.all_gather(factor_peer, "grp", axis=1, tiled=True),
        factor_own,
        (((0,), (0,)), ((), ())),
        precision=lax.Precision.HIGHEST,
    )
    front = assembled - weights * product
    return (front, factor_part)


def solution(mesh):
    placed = (P("grp", "row", "col"), P(), P("row", None), P())
    return jax.shard_map(
        per_device,
        mesh=mesh,
        in_specs=placed,
        out_specs=(P("row", ("grp", "col")), P("row", ("grp", "col"))),
        check_vma=False,
    )
```

profile of v0, /device:TPU:7, one launch (start us, length us, event | category | flops | bytes accessed | tf_op | source)
XLA Modules:
  0.0 684.9 jit_solution(15058187260444157115)
XLA Ops:
  7.2 0.0 copy-start
  7.2 9.7 %copy.7 = f32[1,1536,1536]{1,2,0:T(8,128)} copy(f32[1,1536,1536]{2,1,0:T(8,128)} %param.6) | data formatting | bytes 18874368 | tf_op args[0]
  16.9 0.0 copy-start.5
  16.9 12.7 %copy.8 = f32[1536,12,128]{2,1,0:T(8,128)} copy(f32[1536,12,128]{0,2,1:T(8,128)} %bitcast.41) | data formatting | bytes 18874368 | tf_op jit(solution)/shard_map/reshape;squeeze | solution.py:32
  29.7 0.0 copy-done.5
  29.7 0.1 dynamic-slice_subtract_fusion.1
  29.7 14.5 %fusion.4 = f32[8,1536,3,128]{3,0,1,2:T(8,128)} fusion(f32[1536,12,128]{2,1,0:T(8,128)} %copy.8, s32[8,3]{0,1:T(4,128)S(1)} %multiply_add_fusion, s32[12]{0:T(128)S(1)} %fusion.17), kind=kOutput, calls=%fused_computation.4 | convolution fusion | flops 679477504 | bytes 28311696 | tf_op jit(solution)/shard_map/gsq,iqb->gisb/dot_general | solution.py:42
  44.3 18.8 %copy.9 = f32[8,1536,3,128]{1,3,2,0:T(8,128)} copy(f32[8,1536,3,128]{3,0,1,2:T(8,128)} %fusion.4) | data formatting | bytes 37748736 | tf_op jit(solution)/shard_map/gsq,iqb->gisb/transpose | solution.py:42
  63.1 7.5 %all-to-all-start = ((f32[8,1536,384]{1,2,0:T(8,128)}), f32[8,1536,384]{1,2,0:T(8,128)}, u32[]{:S(2)}, u32[]{:S(2)}) async-start(f32[8,1536,384]{1,2,0:T(8,128)} %bitcast.40), calls=%async_computation | async-start | bytes 37748736 | tf_op jit(solution)/shard_map/all_to_all | solution.py:44
  70.6 0.0 all-reduce.4.cloned.1.call-start
  70.6 254.1 %all-to-all-done = f32[8,1536,384]{1,2,0:T(8,128)} async-done(((f32[8,1536,384]{1,2,0:T(8,128)}), f32[8,1536,384]{1,2,0:T(8,128)}, u32[]{:S(2)}, u32[]{:S(2)}) %all-to-all-start) | async-done | bytes 18874400 | tf_op jit(solution)/shard_map/all_to_all | solution.py:44
  324.7 18.7 %copy.10 = f32[8,1536,384]{2,1,0:T(8,128)} copy(f32[8,1536,384]{1,2,0:T(8,128)} %all-to-all-done) | data formatting | bytes 37748736 | tf_op jit(solution)/shard_map/all_to_all | solution.py:44
  343.5 24.3 %fusion.7 = f32[24,128,384]{2,0,1:T(8,128)S(1)} fusion(f32[8,12,128,384]{3,2,1,0:T(8,128)} %bitcast.39, s32[8,12]{1,0:T(8,128)S(1)} %get-tuple-element.18), kind=kOutput, calls=%fused_computation.7 | convolution fusion | flops 1358956800 | bytes 23593344 | tf_op jit(solution)/shard_map/smq,sqbn->mbn/dot_general | solution.py:47
  367.8 0.0 copy-start.1
  367.8 2.2 copy-done.1
  370.0 0.1 slice_select_fusion
  370.1 1.4 copy.14
  371.5 0.0 all-reduce.4.cloned.1.call-update
  371.5 0.0 copy-start.4
  371.5 0.0 all-gather.3.cloned.1.call-start
  371.6 51.3 %all-reduce.4.cloned.1.call-done = f32[1024,384]{1,0:T(8,128)} async-done(((f32[1024,384]{1,0:T(8,128)}), f32[1024,384]{1,0:T(8,128)}) %all-reduce.4.cloned.1.call-update) | async-done | bytes 1572880 | tf_op jit(solution)/shard_map/psum | solution.py:14
  422.9 0.0 copy-done
  422.9 4.8 convolution_bitcast_fusion
  427.7 0.0 all-gather.3.cloned.1.call-update
  427.7 0.0 all-reduce.6.cloned.1.call-start
  427.7 25.9 %all-gather.3.cloned.1.call-done = f32[1024,384]{0,1:T(8,128)} async-done(((f32[256,384]{0,1:T(8,128)}), f32[1024,384]{0,1:T(8,128)}) %all-gather.3.cloned.1.call-update) | async-done | bytes 1572880 | tf_op jit(solution)/shard_map/all_gather | solution.py:51
  453.7 1.4 broadcast_select_fusion
  455.0 0.0 all-reduce.6.cloned.1.call-update
  455.1 0.3 all-gather.5.cloned.1.call-start
  455.3 51.5 %all-reduce.6.cloned.1.call-done = f32[1024,384]{0,1:T(8,128)} async-done(((f32[1024,384]{0,1:T(8,128)}), f32[1024,384]{0,1:T(8,128)}) %all-reduce.6.cloned.1.call-update) | async-done | bytes 1572880 | tf_op jit(solution)/shard_map/psum | solution.py:14
  506.9 0.0 all-gather.5.cloned.1.call-update
  506.9 0.0 copy-done.4
  507.0 0.1 pad_dynamic-slice_fusion
  507.0 0.1 copy.13
  507.1 0.4 broadcast_in_dim.9
  507.5 3.1 copy.25
  510.6 6.0 copy.15
  516.7 0.0 copy-start.3
  516.7 0.0 copy-start.2
  516.7 5.7 copy.12
  522.3 0.0 copy-done.3
  522.4 0.9 copy.16
  523.3 131.2 %all-gather.5.cloned.1.call-done = f32[1024,3072]{0,1:T(8,128)} async-done(((f32[1024,384]{0,1:T(8,128)}), f32[1024,3072]{0,1:T(8,128)}) %all-gather.5.cloned.1.call-update) | async-done | bytes 12582928 | tf_op jit(solution)/shard_map/all_gather | solution.py:63
  654.5 0.0 copy-done.2
  654.5 23.9 %bitcast_subtract_fusion = f32[3072,384]{1,0:T(8,128)} fusion(f32[24,128,384]{2,1,0:T(8,128)} %copy.12, f32[3072,384]{1,0:T(8,128)} %copy.15, f32[1024,3072]{0,1:T(8,128)} %all-gather.5.cloned.1.call-done, f32[1024,384]{0,1:T(8,128)S(1)} %copy-done.2), kind=kOutput, calls=%fused_computation.6 | convolution fusion | flops 14497873920 | bytes 28311552 | tf_op jit(solution)/shard_map/dot_general | solution.py:62
  (3 shorter events, 0.0 us)
Async XLA Ops:
  7.2 415.7 %copy-start = (f32[256,1024]{1,0:T(8,128)S(1)}, f32[256,1024]{1,0:T(8,128)}, u32[]{:S(2)}) copy-start(f32[256,1024]{1,0:T(8,128)} %param.8) | copy-start | bytes 3145732
  16.9 12.7 %copy-start.5 = (s32[8,48]{1,0:T(8,128)S(1)}, s32[8,48]{1,0:T(8,128)}, u32[]{:S(2)}) copy-start(s32[8,48]{1,0:T(8,128)} %param.7) | copy-start | bytes 4612
  63.1 261.7 %all-to-all-start = ((f32[8,1536,384]{1,2,0:T(8,128)}), f32[8,1536,384]{1,2,0:T(8,128)}, u32[]{:S(2)}, u32[]{:S(2)}) async-start(f32[8,1536,384]{1,2,0:T(8,128)} %bitcast.40), calls=%async_computation | async-start | bytes 37748736 | tf_op jit(solution)/shard_map/all_to_all | solution.py:44
  70.6 352.3 %all-reduce.4.cloned.1.call-start = ((), (), s32[]{:S(2)}) async-start(), calls=%async_computation.1 | async-start | bytes 3145728 | tf_op jit(solution)/shard_map/psum | solution.py:14
  367.8 2.2 copy-start.1
  371.5 135.4 %copy-start.4 = (s32[88,88]{1,0:T(8,128)S(1)}, s32[88,88]{1,0:T(8,128)}, u32[]{:S(2)}) copy-start(s32[88,88]{1,0:T(8,128)} %param.9) | copy-start | bytes 92932
  371.5 82.2 %all-gather.3.cloned.1.call-start = ((), (), s32[]{:S(2)}) async-start(), calls=%async_computation.2 | async-start | bytes 1966080 | tf_op jit(solution)/shard_map/all_gather | solution.py:51
  427.7 79.2 %all-reduce.6.cloned.1.call-start = ((), (), s32[]{:S(2)}) async-start(), calls=%async_computation.3 | async-start | bytes 3145728 | tf_op jit(solution)/shard_map/psum | solution.py:14
  455.1 199.4 %all-gather.5.cloned.1.call-start = ((), (), s32[]{:S(2)}) async-start(), calls=%async_computation.4 | async-start | bytes 14155776 | tf_op jit(solution)/shard_map/all_gather | solution.py:63
  516.7 5.7 copy-start.3
  516.7 137.8 %copy-start.2 = (f32[1024,384]{0,1:T(8,128)S(1)}, f32[1024,384]{0,1:T(8,128)}, u32[]{:S(2)}) copy-start(f32[1024,384]{0,1:T(8,128)} %all-gather.3.cloned.1.call-done) | copy-start | bytes 4718596
Sparse Core Ops, SparseCore 0:
  371.6 51.2 all-reduce.3
  427.8 25.8 all-gather.2
  456.1 50.7 all-reduce.5
  509.1 145.3 all-gather.4
where the time goes:
time: 689 us; the launch traced here: 685 us
  waiting for transfers between devices  514 us (75%)
  local copies, waits for them, and re-layouts  79.9 us (12%)
  matrix products  67.4 us (10%)
  between operations  13.9 us (2%)
  starting transfers between devices  7.88 us (1%)
    all_to_all x1, waiting for transfers between devices, per_device(): lax.all_to_all(spread, 'grp', split_axis=0, concat_axis=0, tiled=True)  254 us
    all_gather x1, waiting for transfers between devices, per_device(): lax.all_gather(factor_peer, 'grp', axis=1, tiled=True)  131 us
    psum x2, waiting for transfers between devices, broadcast(): return lax.psum(kept, axis)  103 us
    all_gather x1, waiting for transfers between devices, per_device(): factor_own = lax.all_gather(factor_part, 'row', axis=0, tiled=True)  25.9 us
    dot_general x1, matrix products, per_device(): jnp.einsum('smq,sqbn->mbn', row_select, pieces, precision=lax.Precision.H...  24.3 us
    dot_general x1, matrix products, per_device(): lax.dot_general(lax.all_gather(factor_peer, 'grp', axis=1, tiled=True), f...  23.9 us
    transpose x1, local copies, waits for them, and re-layouts, per_device(): jnp.einsum('gsq,iqb->gisb', col_select, strips, precision=lax.Precision.H...  18.8 us
    all_to_all x1, local copies, waits for them, and re-layouts, per_device(): lax.all_to_all(spread, 'grp', split_axis=0, concat_axis=0, tiled=True)  18.7 us
  transfers between devices with their start and end apart: 5, of which 5 were waited for; matrix products, arithmetic and copies ran while one was open for 2% of the time, Pallas kernels for 0%

commit v1 on v0

v1 whole, which is shorter than its diff:
```python
import functools

import jax
import jax.numpy as jnp
from jax import lax
from jax.experimental import pallas as pl
from jax.experimental.pallas import tpu as pltpu
from jax.sharding import PartitionSpec as P

MESH = pl.DeviceIdType.MESH
B = 128
GROUPS = 8
PB = 24
CB = 12
SH = 3
WT = 8
W = 1024
NX = 4
NY = 4
HALF = 6
HROWS = HALF * B
SLOTS = 2 * HROWS
TILES = 2 * HALF
ZERO = NX * 2 * HALF
NONE = 1000
WIDTH = SH * B
BIG = 3072


def pack_kernel(map_ref, child_ref, pack_ref, rows_ref, cols_ref, held, in_sems, sems):
    g = lax.axis_index("grp")
    r = lax.axis_index("row")
    c = lax.axis_index("col")
    x, zh = g // 2, lax.rem(g, 2)
    loads = []
    for n in range(4):
        span = pl.ds(n * HROWS // 2, HROWS // 2)
        loads.append(pltpu.make_async_copy(child_ref.at[span, :], held.at[span, :], in_sems.at[n]))
        loads[n].start()

    @pl.loop(0, 2 * NX * PB)
    def _(i):
        rows_ref[i] = jnp.int32(NONE)

    for i in range(2 * NX * 4):
        cols_ref[i] = jnp.int32(NONE)

    @pl.loop(0, NX)
    def _(s):
        child = 2 * s + zh
        for a in range(CB):
            i = map_ref[child, r * CB + a] - r * PB
            rows_ref[(a // HALF) * NX * PB + s * PB + i] = jnp.int32(a % HALF)
        for d in range(2):
            mine = 2 * x + (zh if d == 0 else 1 - zh)
            before = jnp.int32(-1)
            for q in range(CB):
                p = map_ref[child, c * CB + q] - c * PB
                owner = p // SH
                slot = jnp.where(owner == before, 1, 0)
                before = owner
                j = jnp.where(owner == mine, p - owner * SH, 3)
                cols_ref[d * NX * 4 + s * 4 + j] = (s * 2 + slot) * HALF

    owners, slots = [], []
    for q in range(CB):
        owners.append((map_ref[g, c * CB + q] - c * PB) // SH)
        slots.append(jnp.where(owners[q] == owners[q - 1], 1, 0) if q else jnp.int32(0))
    copies = []
    for h in range(2):
        loads[2 * h].wait()
        loads[2 * h + 1].wait()
        for q in range(CB):
            copy = pltpu.make_async_copy(
                held.at[pl.ds(h * HROWS, HROWS), pl.ds(q * B, B)],
                pack_ref.at[h, owners[q], pl.ds(pl.multiple_of(slots[q] * HROWS, HROWS), HROWS), :],
                sems.at[h, q],
            )
            copy.start()
            copies.append(copy)
    for copy in copies:
        copy.wait()


def front_kernel(
    rows_ref, cols_ref, pattern_ref, pack_ref, inverse_ref,
    front_ref, panel_ref,
    as_ref, ao_ref, bs_ref, bo_ref,
    out_part, in_part, product, product_out,
    own, own_hi, own_lo, near, far,
    inverse_all, top_hi, top_lo,
    x_send, x_recv, x_local, z_send, z_recv, i_send, i_recv, i_local,
    r_send, r_recv, y_send, y_recv, n_send, n_recv, n_local, f_send, f_recv,
    p_send, p_recv, go,
):
    g = lax.axis_index("grp")
    r = lax.axis_index("row")
    c = lax.axis_index("col")
    x, zh = g // 2, lax.rem(g, 2)

    def at(grp=None, row=None, col=None):
        return {
            "grp": g if grp is None else grp,
            "row": r if row is None else row,
            "col": c if col is None else col,
        }

    def x_peer(d):
        return at(grp=lax.rem(x + d, NX) * 2 + zh)

    def y_peer(d):
        return at(col=lax.rem(c + d, NY))

    z_peer = at(grp=2 * x + 1 - zh)

    barrier = pltpu.get_barrier_semaphore()
    peers = [x_peer(d) for d in range(1, NX)] + [y_peer(d) for d in range(1, NY)]
    peers += [at(row=lax.rem(r + d, 4)) for d in range(1, 4)] + [z_peer]
    for peer in peers:
        pl.semaphore_signal(barrier, inc=1, device_id=peer, device_id_type=MESH)
    pl.semaphore_wait(barrier, len(peers))

    def remote(src, dst, send, recv, device):
        return pltpu.make_async_remote_copy(
            src_ref=src, dst_ref=dst, send_sem=send, recv_sem=recv,
            device_id=device, device_id_type=MESH,
        )

    chunks = [as_ref, ao_ref, bs_ref, bo_ref]

    def x_copy(k, d):
        owner = lax.rem(x + d, NX) * 2 + (zh if k % 2 == 0 else 1 - zh)
        return remote(
            pack_ref.at[k // 2, owner],
            chunks[k].at[pl.ds(x * TILES, TILES)],
            x_send.at[k * 3 + d - 1], x_recv.at[k * 3 + d - 1], x_peer(d),
        )

    def x_arrival(k, d):
        source = lax.rem(x + NX - d, NX)
        return remote(
            pack_ref.at[k // 2, 0],
            chunks[k].at[pl.ds(source * TILES, TILES)],
            x_send.at[k * 3 + d - 1], x_recv.at[k * 3 + d - 1], x_peer(NX - d),
        )

    def x_own(k):
        owner = 2 * x + (zh if k % 2 == 0 else 1 - zh)
        return pltpu.make_async_copy(
            pack_ref.at[k // 2, owner],
            chunks[k].at[pl.ds(x * TILES, TILES)],
            x_local.at[k],
        )

    def x_start(k):
        for d in (2, 1, 3):
            x_copy(k, d).start()
        x_own(k).start()

    def x_wait(k):
        x_own(k).wait()
        for d in range(1, NX):
            x_arrival(k, d).wait_recv()

    def inverse_copy():
        return remote(
            inverse_ref,
            inverse_all.at[pl.ds(pl.multiple_of(r * 256, 256), 256), :],
            i_send, i_recv.at[r - 1], at(row=0),
        )

    for ref in chunks:
        ref[ZERO] = jnp.zeros((B, B), jnp.float32)

    @pl.when(r == 0)
    def _():
        x_start(1)
        x_start(0)
        pltpu.make_async_copy(inverse_ref, inverse_all.at[pl.ds(0, 256), :], i_local).start()

    @pl.when(r > 0)
    def _():
        inverse_copy().start()

    @pl.when(r > 1)
    def _():
        x_start(1)
        x_start(3)
        x_start(0)
        x_start(2)

    def tile(d, i, j, use):
        total = None
        for s in range(NX):
            for h, ref in use:
                index = jnp.minimum(
                    rows_ref[h * NX * PB + s * PB + i] + cols_ref[d * NX * 4 + s * 4 + j], ZERO
                )
                value = ref[index]
                total = value if total is None else total + value
        return total

    def spread(first, last, d, put):
        a_ref, b_ref = (as_ref, bs_ref) if d == 0 else (ao_ref, bo_ref)
        for low, high, use in (
            (0, 9, ((0, a_ref),)),
            (9, 15, ((0, a_ref), (1, b_ref))),
            (15, 24, ((1, b_ref),)),
        ):
            low, high = max(low, first), min(high, last)
            if low < high:

                @pl.loop(low, high)
                def _(i):
                    for j in range(SH):
                        put(i, j, tile(d, i, j, use))

    def rows_of(i):
        return pl.ds(pl.multiple_of(i * B, B), B)

    def put_out(i, j, value):
        out_part[rows_of(i), j * B : (j + 1) * B] = value

    def z_copy(part):
        span = pl.ds(0, W) if part == 0 else pl.ds(W, BIG - W)
        return remote(
            out_part.at[span, :], in_part.at[span, :],
            z_send.at[part], z_recv.at[part], z_peer,
        )

    def own_tile(ref, col, j):
        return ref.at[pl.ds(pl.multiple_of(col * WIDTH + j * B, B), B), :]

    def r_copy(j, d):
        return remote(
            own_tile(own, c, j), own_tile(own, c, j),
            r_send.at[(d - 1) * 3 + j], r_recv.at[j], at(row=r + d),
        )

    def y_copy(j, d):
        return remote(
            own_tile(own, c, j), own_tile(own, c, j),
            y_send.at[(d - 1) * 3 + j], y_recv.at[(d - 1) * 3 + j], y_peer(d),
        )

    def y_arrival(j, d):
        source = lax.rem(c + NY - d, NY)
        return remote(
            own_tile(own, source, j), own_tile(own, source, j),
            y_send.at[(d - 1) * 3 + j], y_recv.at[(d - 1) * 3 + j], y_peer(NY - d),
        )

    @pl.when(r == 0)
    def _():
        x_wait(1)
        spread(0, WT, 1, put_out)
        z_copy(0).start()
        x_wait(0)
        pl.semaphore_signal(go, inc=1, device_id=at(row=1), device_id_type=MESH)
        x_start(3)
        x_start(2)

        def put_top(i, j, value):
            product[rows_of(i), j * B : (j + 1) * B] = value

        spread(0, WT, 0, put_top)
        for k in range(1, 4):
            remote(
                inverse_ref, inverse_all.at[pl.ds(k * 256, 256), :],
                i_send, i_recv.at[k - 1], at(row=k),
            ).wait_recv()
        pltpu.make_async_copy(inverse_ref, inverse_all.at[pl.ds(0, 256), :], i_local).wait()
        z_copy(0).wait_recv()

        @pl.loop(0, WT)
        def _(i):
            value = product[rows_of(i), :] + in_part[rows_of(i), :]
            high = value.astype(jnp.bfloat16)
            top_hi[rows_of(i), :] = high
            top_lo[rows_of(i), :] = (value - high.astype(jnp.float32)).astype(jnp.bfloat16)

        for k in range(4):
            block = inverse_all[k * 256 : (k + 1) * 256, :]
            high = block.astype(jnp.bfloat16)
            low = (block - high.astype(jnp.float32)).astype(jnp.bfloat16)
            dot = functools.partial(jnp.dot, preferred_element_type=jnp.float32)
            part = dot(high, top_lo[...]) + dot(low, top_hi[...]) + dot(high, top_hi[...])
            own[pl.ds(pl.multiple_of(c * WIDTH, WIDTH), WIDTH), k * 256 : (k + 1) * 256] = part.T
        for j in range(SH):
            r_copy(j, 1).start()
            r_copy(j, 2).start()
            for d in range(1, NY):
                y_copy(j, d).start()

    @pl.when(r == 1)
    def _():
        pl.semaphore_wait(go, 1)
        x_start(1)
        x_start(3)
        x_start(0)
        x_start(2)

    @pl.when(r > 1)
    def _():
        x_wait(1)
        spread(0, WT, 1, put_out)
        z_copy(0).start()

    @pl.when(r > 0)
    def _():
        for j in range(SH):
            remote(
                own_tile(own, c, j), own_tile(own, c, j),
                r_send.at[j], r_recv.at[j], at(row=r - 1),
            ).wait_recv()

            @pl.when(r == 2)
            def _():
                r_copy(j, 1).start()

            for d in range(1, NY):
                y_copy(j, d).start()

    @pl.when(r == 1)
    def _():
        x_wait(1)
        spread(0, WT, 1, put_out)
        z_copy(0).start()

    x_wait(3)
    spread(WT, PB, 1, put_out)
    z_copy(1).start()

    panel_ref[...] = own[
        pl.ds(pl.multiple_of(c * WIDTH, WIDTH), WIDTH), pl.ds(pl.multiple_of(r * 256, 256), 256)
    ].T

    def n_copy(j):
        return remote(
            own_tile(own, r, j), near.at[pl.ds(j * B, B), :],
            n_send.at[j], n_recv.at[j], at(grp=lax.rem(x + NX - c, NX) * 2 + zh),
        )

    def n_arrival(j):
        return remote(
            own_tile(own, r, j), near.at[pl.ds(j * B, B), :],
            n_send.at[j], n_recv.at[j], at(grp=lax.rem(x + c, NX) * 2 + zh),
        )

    def n_own(j):
        return pltpu.make_async_copy(own_tile(own, r, j), near.at[pl.ds(j * B, B), :], n_local.at[j])

    def f_copy(j):
        return remote(
            near.at[pl.ds(j * B, B), :], far.at[pl.ds(j * B, B), :],
            f_send.at[j], f_recv.at[j], z_peer,
        )

    for j in range(SH):
        for d in range(1, NY):

            @pl.when(lax.rem(c + NY - r, NY) == d)
            def _():
                y_arrival(j, d).wait_recv()

        @pl.when(c > 0)
        def _():
            n_copy(j).start()

        @pl.when(c == 0)
        def _():
            n_own(j).start()

    for j in range(SH):

        @pl.when(c > 0)
        def _():
            n_arrival(j).wait_recv()

        @pl.when(c == 0)
        def _():
            n_own(j).wait()

        f_copy(j).start()

    for j in range(SH):
        for d in range(1, NY):

            @pl.when(lax.rem(c + NY - r, NY) != d)
            def _():
                y_arrival(j, d).wait_recv()

    @pl.loop(0, NY * SH)
    def _(t):
        value = own[rows_of(t), :]
        high = value.astype(jnp.bfloat16)
        own_hi[rows_of(t), :] = high
        own_lo[rows_of(t), :] = (value - high.astype(jnp.float32)).astype(jnp.bfloat16)

    def place(b, j):
        return 3 * (2 * lax.rem(x + c, NX) + (zh if b == 0 else 1 - zh)) + j

    def p_copy(b, j, d):
        n = (b * 3 + j) * 3 + d - 1
        return remote(
            product_out.at[pl.ds(n * B, B), :], product.at[rows_of(place(b, j)), :],
            p_send.at[n], p_recv.at[n], y_peer(d),
        )

    def p_arrival(b, j, d):
        n = (b * 3 + j) * 3 + d - 1
        source = lax.rem(c + NY - d, NY)
        index = 3 * (2 * lax.rem(x + source, NX) + (zh if b == 0 else 1 - zh)) + j
        return remote(
            product_out.at[pl.ds(n * B, B), :], product.at[rows_of(index), :],
            p_send.at[n], p_recv.at[n], y_peer(NY - d),
        )

    def times(a, b):
        return lax.dot_general(a, b, (((1,), (1,)), ((), ())), preferred_element_type=jnp.float32)

    for b in range(2):
        for j in range(SH):
            if b == 1:
                f_copy(j).wait_recv()
            value = (near, far)[b][j * B : (j + 1) * B, :]
            high = value.astype(jnp.bfloat16)
            low = (value - high.astype(jnp.float32)).astype(jnp.bfloat16)
            for d in (2, 1, 3, 0):
                col = lax.rem(c + d, NY)
                span = pl.ds(pl.multiple_of(col * WIDTH, WIDTH), WIDTH)
                got = (
                    times(high, own_lo[span, :]) + times(low, own_hi[span, :])
                    + times(high, own_hi[span, :])
                )
                if d == 0:
                    product[rows_of(place(b, j)), :] = got
                else:
                    n = (b * 3 + j) * 3 + d - 1
                    product_out[n * B : (n + 1) * B, :] = got
                    p_copy(b, j, d).start()

    @pl.when(r > 0)
    def _():
        x_wait(0)

    x_wait(2)

    @pl.when(r > 0)
    def _():
        z_copy(0).wait_recv()

    z_copy(1).wait_recv()
    for b in range(2):
        for j in range(SH):
            for d in range(1, NY):
                p_arrival(b, j, d).wait_recv()

    def put_front(i, j, value):
        down = r * PB + i - WT
        right = c * PB + g * SH + j - WT
        weight = pattern_ref[jnp.maximum(down, 0), jnp.maximum(right, 0)]
        weight = jnp.where((down >= 0) & (right >= 0), weight, 0).astype(jnp.float32)
        span = (rows_of(i), slice(j * B, (j + 1) * B))
        front_ref[span] = value + in_part[span] - weight * product[span]

    spread(0, PB, 0, put_front)

    for k in range(4):
        for d in range(1, NX):
            x_copy(k, d).wait_send()
    for part in range(2):
        z_copy(part).wait_send()

    @pl.when(r > 0)
    def _():
        inverse_copy().wait_send()

    for j in range(SH):

        @pl.when((r == 0) | (r == 2))
        def _():
            r_copy(j, 1).wait_send()

        @pl.when(r == 0)
        def _():
            r_copy(j, 2).wait_send()

        for d in range(1, NY):
            y_copy(j, d).wait_send()

        @pl.when(c > 0)
        def _():
            n_copy(j).wait_send()

        f_copy(j).wait_send()
        for b in range(2):
            for d in range(1, NY):
                p_copy(b, j, d).wait_send()


def per_device(children, child_map, panel_inverse, pattern):
    anywhere = pl.BlockSpec(memory_space=pl.ANY)
    smem = pl.BlockSpec(memory_space=pltpu.SMEM)
    vmem = pl.BlockSpec(memory_space=pltpu.VMEM)
    pack, rows, cols = pl.pallas_call(
        pack_kernel,
        name="pack",
        out_shape=(
            jax.ShapeDtypeStruct((2, GROUPS, SLOTS, B), jnp.float32),
            jax.ShapeDtypeStruct((2 * NX * PB,), jnp.int32),
            jax.ShapeDtypeStruct((2 * NX * 4,), jnp.int32),
        ),
        in_specs=[smem, anywhere],
        out_specs=(anywhere, smem, smem),
        scratch_shapes=[
            pltpu.VMEM((CB * B, CB * B), jnp.float32),
            pltpu.SemaphoreType.DMA((4,)),
            pltpu.SemaphoreType.DMA((2, CB)),
        ],
        compiler_params=pltpu.CompilerParams(vmem_limit_bytes=16 * 2**20),
    )(child_map, children[0])
    pack = pack.reshape(2, GROUPS, TILES, B, B)
    f32, bf16 = jnp.float32, jnp.bfloat16
    dma = pltpu.SemaphoreType.DMA
    chunk = pltpu.VMEM((ZERO + 1, B, B), f32)
    return pl.pallas_call(
        front_kernel,
        name="front",
        out_shape=(
            jax.ShapeDtypeStruct((BIG, WIDTH), f32),
            jax.ShapeDtypeStruct((256, WIDTH), f32),
        ),
        in_specs=[smem, smem, smem, anywhere, anywhere],
        out_specs=(vmem, vmem),
        scratch_shapes=[
            chunk, chunk, chunk, chunk,
            pltpu.VMEM((BIG, WIDTH), f32), pltpu.VMEM((BIG, WIDTH), f32),
            pltpu.VMEM((BIG, WIDTH), f32), pltpu.VMEM((18 * B, WIDTH), f32),
            pltpu.VMEM((NY * WIDTH, W), f32),
            pltpu.VMEM((NY * WIDTH, W), bf16), pltpu.VMEM((NY * WIDTH, W), bf16),
            pltpu.VMEM((WIDTH, W), f32), pltpu.VMEM((WIDTH, W), f32),
            pltpu.VMEM((W, W), f32),
            pltpu.VMEM((W, WIDTH), bf16), pltpu.VMEM((W, WIDTH), bf16),
            dma((12,)), dma((12,)), dma((4,)), dma((2,)), dma((2,)), dma(()), dma((3,)), dma(()),
            dma((6,)), dma((3,)), dma((9,)), dma((9,)), dma((3,)), dma((3,)), dma((3,)), dma((3,)), dma((3,)),
            dma((18,)), dma((18,)), pltpu.SemaphoreType.REGULAR,
        ],
        compiler_params=pltpu.CompilerParams(
            collective_id=1, has_side_effects=True, vmem_limit_bytes=62 * 2**20
        ),
    )(rows, cols, pattern, pack, panel_inverse)


def solution(mesh):
    placed = (P("grp", "row", "col"), P(), P("row", None), P())
    return jax.shard_map(
        per_device,
        mesh=mesh,
        in_specs=placed,
        out_specs=(P("row", ("grp", "col")), P("row", ("grp", "col"))),
        check_vma=False,
    )
```

time: 689 us -> 261 us (0.38)
  the two profiles are of different devices: /device:TPU:7 before, /device:TPU:33 now
where the time goes in v1:
time: 261 us; the launch traced here: 260 us
  Pallas kernels  244 us (93%)
  local copies, waits for them, and re-layouts  15.6 us (6%)
    pallas_call x1, Pallas kernels, per_device(): pl.pallas_call(front_kernel, name='front', out_shape=(jax.ShapeDtypeStruc...  238 us
    unnamed x14, local copies, waits for them, and re-layouts  15.6 us
    pallas_call x1, Pallas kernels, per_device(): pl.pallas_call(pack_kernel, name='pack', out_shape=(jax.ShapeDtypeStruct(...  5.92 us

profile of v1, /device:TPU:33, one launch (start us, length us, event | category | flops | bytes accessed | tf_op | source)
XLA Modules:
  0.0 260.3 jit_solution(7974207836290128832)
XLA Ops:
  0.6 0.0 copy-start.1
  0.6 3.7 %copy-done.1 = f32[1,1536,1536]{2,1,0:T(8,128)S(1)} copy-done((f32[1,1536,1536]{2,1,0:T(8,128)S(1)}, f32[1,1536,1536]{2,1,0:T(8,128)}, u32[]{:S(2)}) %copy-start.1) | copy-done | bytes 9437208
  4.3 0.0 copy-start.2
  4.3 0.7 copy-done.2
  5.0 5.9 %pack.1 = (f32[2,8,1536,128]{3,2,1,0:T(8,128)S(1)}, s32[192]{0:T(256)S(1)}, s32[32]{0:T(128)S(1)}) custom-call(s32[8,48]{1,0:T(8,128)S(1)} %copy-done.2, f32[1536,1536]{1,0:T(8,128)S(1)} %bitcast.3), custom_call_target="tpu_custom_call" | custom-call | tf_op jit(solution)/shard_map/pack/pallas_call | solution.py:506
  10.9 0.0 copy-start
  10.9 4.5 %copy-done = f32[2,8,1536,128]{3,2,1,0:T(8,128)} copy-done((f32[2,8,1536,128]{3,2,1,0:T(8,128)}, f32[2,8,1536,128]{3,2,1,0:T(8,128)S(1)}, u32[]{:S(2)}) %copy-start) | copy-done | bytes 12582936
  15.5 0.0 copy-start.3
  15.5 0.6 copy-done.3
  16.0 0.0 copy-start.4
  16.0 0.5 copy-done.4
  16.5 238.1 %front.1 = (f32[3072,384]{1,0:T(8,128)}, f32[256,384]{1,0:T(8,128)}) custom-call(s32[192]{0:T(256)} %copy-done.3, s32[32]{0:T(128)} %copy-done.4, s32[88,88]{1,0:T(8,128)} %pattern_ref.1, f32[2,8,12,128,128]{4,3,2,1,0:T(8,128)} %bitcast.2, f32[256,1024]{1,0:T(8,128)} %inverse_ref.1), custom_call_target="tpu_custom_call" | custom-call | tf_op jit(solution)/shard_map/front/pallas_call | solution.py:527
  254.7 0.0 copy-start.5
  254.7 4.9 %copy.8 = f32[3072,384]{1,0:T(8,128)} copy(f32[3072,384]{1,0:T(8,128)} %get-tuple-element.10) | data formatting | bytes 9437184
  259.6 0.0 copy-done.5
  259.6 0.7 copy.9
Async XLA Ops:
  0.6 3.7 %copy-start.1 = (f32[1,1536,1536]{2,1,0:T(8,128)S(1)}, f32[1,1536,1536]{2,1,0:T(8,128)}, u32[]{:S(2)}) copy-start(f32[1,1536,1536]{2,1,0:T(8,128)} %param.4) | copy-start | bytes 28311556
  4.3 0.7 copy-start.2
  10.9 4.5 %copy-start = (f32[2,8,1536,128]{3,2,1,0:T(8,128)}, f32[2,8,1536,128]{3,2,1,0:T(8,128)S(1)}, u32[]{:S(2)}) copy-start(f32[2,8,1536,128]{3,2,1,0:T(8,128)S(1)} %get-tuple-element.7) | copy-start | bytes 37748740
  15.5 0.6 copy-start.3
  16.0 0.5 copy-start.4
  254.7 4.9 %copy-start.5 = (f32[256,384]{1,0:T(8,128)S(1)}, f32[256,384]{1,0:T(8,128)}, u32[]{:S(2)}) copy-start(f32[256,384]{1,0:T(8,128)} %get-tuple-element.11) | copy-start | bytes 1179652

commit v2 on v1

--- a/solution.py
+++ b/solution.py
@@ -90,7 +90,7 @@
     own, own_hi, own_lo, near, far,
     inverse_all, top_hi, top_lo,
     x_send, x_recv, x_local, z_send, z_recv, i_send, i_recv, i_local,
-    r_send, r_recv, y_send, y_recv, n_send, n_recv, n_local, f_send, f_recv,
+    r_send, r_recv, c_send, c_recv, y_send, y_recv, n_send, n_recv, n_local, f_send, f_recv,
     p_send, p_recv, go,
 ):
     g = lax.axis_index("grp")
@@ -112,6 +112,8 @@
         return at(col=lax.rem(c + d, NY))
 
     z_peer = at(grp=2 * x + 1 - zh)
+    core = lax.rem(r, 2)
+    other_core = at(row=r + 1 - 2 * core)
 
     barrier = pltpu.get_barrier_semaphore()
     peers = [x_peer(d) for d in range(1, NX)] + [y_peer(d) for d in range(1, NY)]
@@ -186,8 +188,6 @@
     def _():
         x_start(1)
         x_start(3)
-        x_start(0)
-        x_start(2)
 
     def tile(d, i, j, use):
         total = None
@@ -222,7 +222,7 @@
         out_part[rows_of(i), j * B : (j + 1) * B] = value
 
     def z_copy(part):
-        span = pl.ds(0, W) if part == 0 else pl.ds(W, BIG - W)
+        span = pl.ds(part * W, W)
         return remote(
             out_part.at[span, :], in_part.at[span, :],
             z_send.at[part], z_recv.at[part], z_peer,
@@ -231,24 +231,31 @@
     def own_tile(ref, col, j):
         return ref.at[pl.ds(pl.multiple_of(col * WIDTH + j * B, B), B), :]
 
+    def own_half(col, j, k):
+        start = col * WIDTH + j * B + k * (B // 2)
+        return own.at[pl.ds(pl.multiple_of(start, B // 2), B // 2), :]
+
     def r_copy(j, d):
-        return remote(
-            own_tile(own, c, j), own_tile(own, c, j),
-            r_send.at[(d - 1) * 3 + j], r_recv.at[j], at(row=r + d),
-        )
+        part = own_tile(own, c, j) if d == 1 else own_half(c, j, d - 2)
+        return remote(part, part, r_send.at[(d - 1) * 3 + j], r_recv.at[j], at(row=d))
+
+    def c_copy(j, d):
+        part = own_half(lax.rem(c + NY - d, NY), j, core)
+        return remote(part, part, c_send.at[d * 3 + j], c_recv.at[d * 3 + j], other_core)
+
+    def c_arrival(j, d):
+        part = own_half(lax.rem(c + NY - d, NY), j, 1 - core)
+        return remote(part, part, c_send.at[d * 3 + j], c_recv.at[d * 3 + j], other_core)
 
     def y_copy(j, d):
-        return remote(
-            own_tile(own, c, j), own_tile(own, c, j),
-            y_send.at[(d - 1) * 3 + j], y_recv.at[(d - 1) * 3 + j], y_peer(d),
-        )
+        part = own_half(c, j, core)
+        n = (d - 1) * 3 + j
+        return remote(part, part, y_send.at[n], y_recv.at[n], y_peer(d))
 
     def y_arrival(j, d):
-        source = lax.rem(c + NY - d, NY)
-        return remote(
-            own_tile(own, source, j), own_tile(own, source, j),
-            y_send.at[(d - 1) * 3 + j], y_recv.at[(d - 1) * 3 + j], y_peer(NY - d),
-        )
+        part = own_half(lax.rem(c + NY - d, NY), j, core)
+        n = (d - 1) * 3 + j
+        return remote(part, part, y_send.at[n], y_recv.at[n], y_peer(NY - d))
 
     @pl.when(r == 0)
     def _():
@@ -258,7 +265,6 @@
         x_wait(0)
         pl.semaphore_signal(go, inc=1, device_id=at(row=1), device_id_type=MESH)
         x_start(3)
-        x_start(2)
 
         def put_top(i, j, value):
             product[rows_of(i), j * B : (j + 1) * B] = value
@@ -287,8 +293,9 @@
             part = dot(high, top_lo[...]) + dot(low, top_hi[...]) + dot(high, top_hi[...])
             own[pl.ds(pl.multiple_of(c * WIDTH, WIDTH), WIDTH), k * 256 : (k + 1) * 256] = part.T
         for j in range(SH):
+            r_copy(j, 2).start()
+            r_copy(j, 3).start()
             r_copy(j, 1).start()
-            r_copy(j, 2).start()
             for d in range(1, NY):
                 y_copy(j, d).start()
 
@@ -297,8 +304,6 @@
         pl.semaphore_wait(go, 1)
         x_start(1)
         x_start(3)
-        x_start(0)
-        x_start(2)
 
     @pl.when(r > 1)
     def _():
@@ -306,20 +311,21 @@
         spread(0, WT, 1, put_out)
         z_copy(0).start()
 
-    @pl.when(r > 0)
-    def _():
-        for j in range(SH):
-            remote(
-                own_tile(own, c, j), own_tile(own, c, j),
-                r_send.at[j], r_recv.at[j], at(row=r - 1),
-            ).wait_recv()
-
-            @pl.when(r == 2)
-            def _():
-                r_copy(j, 1).start()
-
+    @pl.when(r == 1)
+    def _():
+        for j in range(SH):
+            r_copy(j, 1).wait_recv()
             for d in range(1, NY):
                 y_copy(j, d).start()
+
+    @pl.when(r > 1)
+    def _():
+        for j in range(SH):
+            part = own_half(c, j, core)
+            remote(part, part, r_send.at[j], r_recv.at[j], at(row=0)).wait_recv()
+            for d in range(1, NY):
+                y_copy(j, d).start()
+            c_copy(j, 0).start()
 
     @pl.when(r == 1)
     def _():
@@ -328,23 +334,30 @@
         z_copy(0).start()
 
     x_wait(3)
-    spread(WT, PB, 1, put_out)
+
+    @pl.when(r > 0)
+    def _():
+        x_start(0)
+
+    spread(WT, 2 * WT, 1, put_out)
     z_copy(1).start()
 
-    panel_ref[...] = own[
-        pl.ds(pl.multiple_of(c * WIDTH, WIDTH), WIDTH), pl.ds(pl.multiple_of(r * 256, 256), 256)
-    ].T
+
+    @pl.when(r > 1)
+    def _():
+        for j in range(SH):
+            c_arrival(j, 0).wait_recv()
 
     def n_copy(j):
         return remote(
             own_tile(own, r, j), near.at[pl.ds(j * B, B), :],
-            n_send.at[j], n_recv.at[j], at(grp=lax.rem(x + NX - c, NX) * 2 + zh),
+            n_send.at[j], n_recv.at[j], at(grp=lax.rem(x + 2 * NX - c - j, NX) * 2 + zh),
         )
 
     def n_arrival(j):
         return remote(
             own_tile(own, r, j), near.at[pl.ds(j * B, B), :],
-            n_send.at[j], n_recv.at[j], at(grp=lax.rem(x + c, NX) * 2 + zh),
+            n_send.at[j], n_recv.at[j], at(grp=lax.rem(x + c + j, NX) * 2 + zh),
         )
 
     def n_own(j):
@@ -357,38 +370,46 @@
         )
 
     for j in range(SH):
+        for d in (1, 3, 2):
+            y_arrival(j, d).wait_recv()
+            c_copy(j, d).start()
         for d in range(1, NY):
 
             @pl.when(lax.rem(c + NY - r, NY) == d)
             def _():
-                y_arrival(j, d).wait_recv()
-
-        @pl.when(c > 0)
+                c_arrival(j, d).wait_recv()
+
+        @pl.when(lax.rem(c + j, NX) > 0)
         def _():
             n_copy(j).start()
 
-        @pl.when(c == 0)
+        @pl.when(lax.rem(c + j, NX) == 0)
         def _():
             n_own(j).start()
 
+    x_start(2)
+
     for j in range(SH):
 
-        @pl.when(c > 0)
+        @pl.when(lax.rem(c + j, NX) > 0)
         def _():
             n_arrival(j).wait_recv()
 
-        @pl.when(c == 0)
+        @pl.when(lax.rem(c + j, NX) == 0)
         def _():
             n_own(j).wait()
 
         f_copy(j).start()
+
+    spread(2 * WT, PB, 1, put_out)
+    z_copy(2).start()
 
     for j in range(SH):
         for d in range(1, NY):
 
             @pl.when(lax.rem(c + NY - r, NY) != d)
             def _():
-                y_arrival(j, d).wait_recv()
+                c_arrival(j, d).wait_recv()
 
     @pl.loop(0, NY * SH)
     def _(t):
@@ -398,7 +419,7 @@
         own_lo[rows_of(t), :] = (value - high.astype(jnp.float32)).astype(jnp.bfloat16)
 
     def place(b, j):
-        return 3 * (2 * lax.rem(x + c, NX) + (zh if b == 0 else 1 - zh)) + j
+        return 3 * (2 * lax.rem(x + c + j, NX) + (zh if b == 0 else 1 - zh)) + j
 
     def p_copy(b, j, d):
         n = (b * 3 + j) * 3 + d - 1
@@ -410,7 +431,7 @@
     def p_arrival(b, j, d):
         n = (b * 3 + j) * 3 + d - 1
         source = lax.rem(c + NY - d, NY)
-        index = 3 * (2 * lax.rem(x + source, NX) + (zh if b == 0 else 1 - zh)) + j
+        index = 3 * (2 * lax.rem(x + source + j, NX) + (zh if b == 0 else 1 - zh)) + j
         return remote(
             product_out.at[pl.ds(n * B, B), :], product.at[rows_of(index), :],
             p_send.at[n], p_recv.at[n], y_peer(NY - d),
@@ -440,6 +461,10 @@
                     product_out[n * B : (n + 1) * B, :] = got
                     p_copy(b, j, d).start()
 
+    panel_ref[...] = own[
+        pl.ds(pl.multiple_of(c * WIDTH, WIDTH), WIDTH), pl.ds(pl.multiple_of(r * 256, 256), 256)
+    ].T
+
     @pl.when(r > 0)
     def _():
         x_wait(0)
@@ -451,25 +476,33 @@
         z_copy(0).wait_recv()
 
     z_copy(1).wait_recv()
+    z_copy(2).wait_recv()
+
+    def put_front(i, j, value):
+        span = (rows_of(i), slice(j * B, (j + 1) * B))
+        front_ref[span] = value + in_part[span]
+
+    spread(0, PB, 0, put_front)
+
     for b in range(2):
         for j in range(SH):
             for d in range(1, NY):
                 p_arrival(b, j, d).wait_recv()
 
-    def put_front(i, j, value):
-        down = r * PB + i - WT
-        right = c * PB + g * SH + j - WT
-        weight = pattern_ref[jnp.maximum(down, 0), jnp.maximum(right, 0)]
-        weight = jnp.where((down >= 0) & (right >= 0), weight, 0).astype(jnp.float32)
-        span = (rows_of(i), slice(j * B, (j + 1) * B))
-        front_ref[span] = value + in_part[span] - weight * product[span]
-
-    spread(0, PB, 0, put_front)
+    @pl.loop(0, PB)
+    def _(i):
+        for j in range(SH):
+            down = r * PB + i - WT
+            right = c * PB + g * SH + j - WT
+            weight = pattern_ref[jnp.maximum(down, 0), jnp.maximum(right, 0)]
+            weight = jnp.where((down >= 0) & (right >= 0), weight, 0).astype(jnp.float32)
+            span = (rows_of(i), slice(j * B, (j + 1) * B))
+            front_ref[span] = front_ref[span] - weight * product[span]
 
     for k in range(4):
         for d in range(1, NX):
             x_copy(k, d).wait_send()
-    for part in range(2):
+    for part in range(3):
         z_copy(part).wait_send()
 
     @pl.when(r > 0)
@@ -478,18 +511,20 @@
 
     for j in range(SH):
 
-        @pl.when((r == 0) | (r == 2))
-        def _():
-            r_copy(j, 1).wait_send()
-
         @pl.when(r == 0)
         def _():
-            r_copy(j, 2).wait_send()
+            for d in range(1, 4):
+                r_copy(j, d).wait_send()
+
+        @pl.when(r > 1)
+        def _():
+            c_copy(j, 0).wait_send()
 
         for d in range(1, NY):
             y_copy(j, d).wait_send()
-
-        @pl.when(c > 0)
+            c_copy(j, d).wait_send()
+
+        @pl.when(lax.rem(c + j, NX) > 0)
         def _():
             n_copy(j).wait_send()
 
@@ -518,7 +553,7 @@
             pltpu.SemaphoreType.DMA((4,)),
             pltpu.SemaphoreType.DMA((2, CB)),
         ],
-        compiler_params=pltpu.CompilerParams(vmem_limit_bytes=16 * 2**20),
+        compiler_params=pltpu.CompilerParams(vmem_limit_bytes=60 * 2**20),
     )(child_map, children[0])
     pack = pack.reshape(2, GROUPS, TILES, B, B)
     f32, bf16 = jnp.float32, jnp.bfloat16
@@ -542,8 +577,8 @@
             pltpu.VMEM((WIDTH, W), f32), pltpu.VMEM((WIDTH, W), f32),
             pltpu.VMEM((W, W), f32),
             pltpu.VMEM((W, WIDTH), bf16), pltpu.VMEM((W, WIDTH), bf16),
-            dma((12,)), dma((12,)), dma((4,)), dma((2,)), dma((2,)), dma(()), dma((3,)), dma(()),
-            dma((6,)), dma((3,)), dma((9,)), dma((9,)), dma((3,)), dma((3,)), dma((3,)), dma((3,)), dma((3,)),
+            dma((12,)), dma((12,)), dma((4,)), dma((3,)), dma((3,)), dma(()), dma((3,)), dma(()),
+            dma((9,)), dma((3,)), dma((12,)), dma((12,)), dma((9,)), dma((9,)), dma((3,)), dma((3,)), dma((3,)), dma((3,)), dma((3,)),
             dma((18,)), dma((18,)), pltpu.SemaphoreType.REGULAR,
         ],
         compiler_params=pltpu.CompilerParams(

time: 261 us -> 224 us (0.86)
  the two profiles are of different devices: /device:TPU:33 before, /device:TPU:7 now
where the time goes in v2:
time: 224 us; the launch traced here: 222 us
  Pallas kernels  216 us (96%)
  local copies, waits for them, and re-layouts  5.63 us (3%)
    pallas_call x1, Pallas kernels, per_device(): pl.pallas_call(front_kernel, name='front', out_shape=(jax.ShapeDtypeStruc...  208 us
    pallas_call x1, Pallas kernels, per_device(): pl.pallas_call(pack_kernel, name='pack', out_shape=(jax.ShapeDtypeStruct(...  8.1 us
    unnamed x4, local copies, waits for them, and re-layouts  5.63 us

profile of v2, /device:TPU:7, one launch (start us, length us, event | category | flops | bytes accessed | tf_op | source)
XLA Modules:
  0.0 222.0 jit_solution(382054079461623787)
XLA Ops:
  0.6 8.1 %pack.1 = (f32[2,8,1536,128]{3,2,1,0:T(8,128)}, s32[192]{0:T(256)}, s32[32]{0:T(128)}) custom-call(s32[8,48]{1,0:T(8,128)} %map_ref.1, f32[1536,1536]{1,0:T(8,128)} %bitcast.3), custom_call_target="tpu_custom_call" | custom-call | tf_op jit(solution)/shard_map/pack/pallas_call | solution.py:541
  8.7 207.6 %front.1 = (f32[3072,384]{1,0:T(8,128)}, f32[256,384]{1,0:T(8,128)}) custom-call(s32[192]{0:T(256)} %get-tuple-element.5.rows_ref, s32[32]{0:T(128)} %get-tuple-element.6.cols_ref, s32[88,88]{1,0:T(8,128)} %pattern_ref.1, f32[2,8,12,128,128]{4,3,2,1,0:T(8,128)} %bitcast.2, f32[256,1024]{1,0:T(8,128)} %inverse_ref.1), custom_call_target="tpu_custom_call" | custom-call | tf_op jit(solution)/shard_map/front/pallas_call | solution.py:562
  216.4 0.0 copy-start
  216.4 4.9 %copy.8 = f32[3072,384]{1,0:T(8,128)} copy(f32[3072,384]{1,0:T(8,128)} %get-tuple-element.10) | data formatting | bytes 9437184
  221.3 0.0 copy-done
  221.3 0.7 copy.9
Async XLA Ops:
  216.4 4.9 %copy-start = (f32[256,384]{1,0:T(8,128)S(1)}, f32[256,384]{1,0:T(8,128)}, u32[]{:S(2)}) copy-start(f32[256,384]{1,0:T(8,128)} %get-tuple-element.11) | copy-start | bytes 1179652

commit v3 on v2

--- a/solution.py
+++ b/solution.py
@@ -27,71 +27,17 @@
 BIG = 3072
 
 
-def pack_kernel(map_ref, child_ref, pack_ref, rows_ref, cols_ref, held, in_sems, sems):
-    g = lax.axis_index("grp")
-    r = lax.axis_index("row")
-    c = lax.axis_index("col")
-    x, zh = g // 2, lax.rem(g, 2)
-    loads = []
-    for n in range(4):
-        span = pl.ds(n * HROWS // 2, HROWS // 2)
-        loads.append(pltpu.make_async_copy(child_ref.at[span, :], held.at[span, :], in_sems.at[n]))
-        loads[n].start()
-
-    @pl.loop(0, 2 * NX * PB)
-    def _(i):
-        rows_ref[i] = jnp.int32(NONE)
-
-    for i in range(2 * NX * 4):
-        cols_ref[i] = jnp.int32(NONE)
-
-    @pl.loop(0, NX)
-    def _(s):
-        child = 2 * s + zh
-        for a in range(CB):
-            i = map_ref[child, r * CB + a] - r * PB
-            rows_ref[(a // HALF) * NX * PB + s * PB + i] = jnp.int32(a % HALF)
-        for d in range(2):
-            mine = 2 * x + (zh if d == 0 else 1 - zh)
-            before = jnp.int32(-1)
-            for q in range(CB):
-                p = map_ref[child, c * CB + q] - c * PB
-                owner = p // SH
-                slot = jnp.where(owner == before, 1, 0)
-                before = owner
-                j = jnp.where(owner == mine, p - owner * SH, 3)
-                cols_ref[d * NX * 4 + s * 4 + j] = (s * 2 + slot) * HALF
-
-    owners, slots = [], []
-    for q in range(CB):
-        owners.append((map_ref[g, c * CB + q] - c * PB) // SH)
-        slots.append(jnp.where(owners[q] == owners[q - 1], 1, 0) if q else jnp.int32(0))
-    copies = []
-    for h in range(2):
-        loads[2 * h].wait()
-        loads[2 * h + 1].wait()
-        for q in range(CB):
-            copy = pltpu.make_async_copy(
-                held.at[pl.ds(h * HROWS, HROWS), pl.ds(q * B, B)],
-                pack_ref.at[h, owners[q], pl.ds(pl.multiple_of(slots[q] * HROWS, HROWS), HROWS), :],
-                sems.at[h, q],
-            )
-            copy.start()
-            copies.append(copy)
-    for copy in copies:
-        copy.wait()
-
-
 def front_kernel(
-    rows_ref, cols_ref, pattern_ref, pack_ref, inverse_ref,
-    front_ref, panel_ref,
+    map_ref, child_ref, inverse_ref,
+    sum_ref, product_ref, panel_ref,
+    rows_ref, cols_ref, held, staged,
     as_ref, ao_ref, bs_ref, bo_ref,
-    out_part, in_part, product, product_out,
+    out_part, in_part, product_out,
     own, own_hi, own_lo, near, far,
     inverse_all, top_hi, top_lo,
-    x_send, x_recv, x_local, z_send, z_recv, i_send, i_recv, i_local,
+    held_sem, x_send, x_recv, z_send, z_recv, i_send, i_recv, i_local,
     r_send, r_recv, c_send, c_recv, y_send, y_recv, n_send, n_recv, n_local, f_send, f_recv,
-    p_send, p_recv, go,
+    p_send, p_recv, p_local, sum_sem, go,
 ):
     g = lax.axis_index("grp")
     r = lax.axis_index("row")
@@ -112,6 +58,14 @@
         return at(col=lax.rem(c + d, NY))
 
     z_peer = at(grp=2 * x + 1 - zh)
+
+    def held_copy(h, q):
+        return pltpu.make_async_copy(
+            child_ref.at[pl.ds(h * HALF, HALF), :, pl.ds(q * B, B)], held.at[q], held_sem.at[h, q]
+        )
+
+    for q in range(CB):
+        held_copy(0, q).start()
     core = lax.rem(r, 2)
     other_core = at(row=r + 1 - 2 * core)
 
@@ -131,9 +85,8 @@
     chunks = [as_ref, ao_ref, bs_ref, bo_ref]
 
     def x_copy(k, d):
-        owner = lax.rem(x + d, NX) * 2 + (zh if k % 2 == 0 else 1 - zh)
-        return remote(
-            pack_ref.at[k // 2, owner],
+        return remote(
+            staged.at[k, d - 1],
             chunks[k].at[pl.ds(x * TILES, TILES)],
             x_send.at[k * 3 + d - 1], x_recv.at[k * 3 + d - 1], x_peer(d),
         )
@@ -141,26 +94,33 @@
     def x_arrival(k, d):
         source = lax.rem(x + NX - d, NX)
         return remote(
-            pack_ref.at[k // 2, 0],
+            staged.at[k, d - 1],
             chunks[k].at[pl.ds(source * TILES, TILES)],
             x_send.at[k * 3 + d - 1], x_recv.at[k * 3 + d - 1], x_peer(NX - d),
         )
 
-    def x_own(k):
-        owner = 2 * x + (zh if k % 2 == 0 else 1 - zh)
-        return pltpu.make_async_copy(
-            pack_ref.at[k // 2, owner],
-            chunks[k].at[pl.ds(x * TILES, TILES)],
-            x_local.at[k],
-        )
+    def pack(k):
+        places = []
+        for d in range(NX):
+            owner = lax.rem(x + d, NX) * 2 + (zh if k % 2 == 0 else 1 - zh)
+            low = c * PB + owner * SH
+            before = sum((map_ref[g, c * CB + q] < low).astype(jnp.int32) for q in range(CB))
+            for slot in range(2):
+                places.append((d, slot, jnp.minimum(before + slot, CB - 1)))
+
+        @pl.loop(0, HALF)
+        def _(a):
+            for d, slot, q in places:
+                if d == 0:
+                    chunks[k][x * TILES + slot * HALF + a] = held[q, a]
+                else:
+                    staged[k, d - 1, slot * HALF + a] = held[q, a]
 
     def x_start(k):
         for d in (2, 1, 3):
             x_copy(k, d).start()
-        x_own(k).start()
 
     def x_wait(k):
-        x_own(k).wait()
         for d in range(1, NX):
             x_arrival(k, d).wait_recv()
 
@@ -176,18 +136,54 @@
 
     @pl.when(r == 0)
     def _():
+        pltpu.make_async_copy(inverse_ref, inverse_all.at[pl.ds(0, 256), :], i_local).start()
+
+    for q in range(CB):
+        held_copy(0, q).wait()
+    pack(1)
+
+    @pl.when(core == 0)
+    def _():
         x_start(1)
+
+    pack(0)
+
+    @pl.when(r == 0)
+    def _():
         x_start(0)
-        pltpu.make_async_copy(inverse_ref, inverse_all.at[pl.ds(0, 256), :], i_local).start()
+
+    for q in range(CB):
+        held_copy(1, q).start()
 
     @pl.when(r > 0)
     def _():
         inverse_copy().start()
 
-    @pl.when(r > 1)
-    def _():
-        x_start(1)
-        x_start(3)
+    for n in range(NX):
+        child = 2 * n + zh
+
+        def place_row(i, at_tile):
+            found = map_ref[child, r * CB + jnp.minimum(at_tile, CB - 1)] == r * PB + i
+            hit = found & (at_tile < CB)
+            rows_ref[n * PB + i] = jnp.where(hit & (at_tile < HALF), at_tile, NONE)
+            rows_ref[(NX + n) * PB + i] = jnp.where(hit & (at_tile >= HALF), at_tile - HALF, NONE)
+            return at_tile + hit.astype(jnp.int32)
+
+        lax.fori_loop(0, PB, place_row, jnp.int32(0))
+        for d in range(2):
+            low = c * PB + (2 * x + (zh if d == 0 else 1 - zh)) * SH
+            slot = jnp.int32(0)
+            for j in range(SH):
+                hit = sum(
+                    (map_ref[child, c * CB + q] == low + j).astype(jnp.int32) for q in range(CB)
+                )
+                cols_ref[(d * NX + n) * 4 + j] = jnp.where(hit > 0, (n * 2 + slot) * HALF, NONE)
+                slot = slot + hit
+
+    for q in range(CB):
+        held_copy(1, q).wait()
+    pack(3)
+    pack(2)
 
     def tile(d, i, j, use):
         total = None
@@ -263,11 +259,13 @@
         spread(0, WT, 1, put_out)
         z_copy(0).start()
         x_wait(0)
-        pl.semaphore_signal(go, inc=1, device_id=at(row=1), device_id_type=MESH)
         x_start(3)
 
+        z_copy(0).wait_recv()
+
         def put_top(i, j, value):
-            product[rows_of(i), j * B : (j + 1) * B] = value
+            span = (rows_of(i), slice(j * B, (j + 1) * B))
+            in_part[span] = in_part[span] + value
 
         spread(0, WT, 0, put_top)
         for k in range(1, 4):
@@ -276,11 +274,10 @@
                 i_send, i_recv.at[k - 1], at(row=k),
             ).wait_recv()
         pltpu.make_async_copy(inverse_ref, inverse_all.at[pl.ds(0, 256), :], i_local).wait()
-        z_copy(0).wait_recv()
 
         @pl.loop(0, WT)
         def _(i):
-            value = product[rows_of(i), :] + in_part[rows_of(i), :]
+            value = in_part[rows_of(i), :]
             high = value.astype(jnp.bfloat16)
             top_hi[rows_of(i), :] = high
             top_lo[rows_of(i), :] = (value - high.astype(jnp.float32)).astype(jnp.bfloat16)
@@ -298,50 +295,65 @@
             r_copy(j, 1).start()
             for d in range(1, NY):
                 y_copy(j, d).start()
-
-    @pl.when(r == 1)
+        x_wait(3)
+        pl.semaphore_signal(go, inc=1, device_id=other_core, device_id_type=MESH)
+
+    def take(d):
+        for j in range(SH):
+            part = own_tile(own, c, j) if d == 1 else own_half(c, j, core)
+            remote(part, part, r_send.at[j], r_recv.at[j], at(row=0)).wait_recv()
+            for d2 in range(1, NY):
+                y_copy(j, d2).start()
+            if d > 1:
+                c_copy(j, 0).start()
+
+    @pl.when(core == 1)
     def _():
         pl.semaphore_wait(go, 1)
         x_start(1)
         x_start(3)
 
-    @pl.when(r > 1)
+    @pl.when(r == 2)
+    def _():
+        x_wait(1)
+        pl.semaphore_signal(go, inc=1, device_id=other_core, device_id_type=MESH)
+        x_start(3)
+        spread(0, WT, 1, put_out)
+        z_copy(0).start()
+        x_wait(3)
+        x_start(0)
+
+    @pl.when(r == 1)
+    def _():
+        take(1)
+
+    @pl.when(core == 1)
     def _():
         x_wait(1)
         spread(0, WT, 1, put_out)
         z_copy(0).start()
 
-    @pl.when(r == 1)
-    def _():
-        for j in range(SH):
-            r_copy(j, 1).wait_recv()
-            for d in range(1, NY):
-                y_copy(j, d).start()
-
-    @pl.when(r > 1)
-    def _():
-        for j in range(SH):
-            part = own_half(c, j, core)
-            remote(part, part, r_send.at[j], r_recv.at[j], at(row=0)).wait_recv()
-            for d in range(1, NY):
-                y_copy(j, d).start()
-            c_copy(j, 0).start()
-
-    @pl.when(r == 1)
-    def _():
-        x_wait(1)
-        spread(0, WT, 1, put_out)
-        z_copy(0).start()
-
-    x_wait(3)
-
-    @pl.when(r > 0)
-    def _():
-        x_start(0)
-
-    spread(WT, 2 * WT, 1, put_out)
-    z_copy(1).start()
-
+    @pl.when(r == 3)
+    def _():
+        take(3)
+
+    @pl.when(core == 1)
+    def _():
+        x_wait(3)
+
+    spread(WT, PB, 1, put_out)
+
+    @pl.when(r != 1)
+    def _():
+        z_copy(1).start()
+
+    @pl.when(core == 0)
+    def _():
+        z_copy(2).start()
+
+    @pl.when(r == 2)
+    def _():
+        take(2)
 
     @pl.when(r > 1)
     def _():
@@ -387,6 +399,10 @@
         def _():
             n_own(j).start()
 
+    @pl.when(core == 1)
+    def _():
+        x_start(0)
+
     x_start(2)
 
     for j in range(SH):
@@ -401,8 +417,13 @@
 
         f_copy(j).start()
 
-    spread(2 * WT, PB, 1, put_out)
-    z_copy(2).start()
+    @pl.when(r == 1)
+    def _():
+        z_copy(1).start()
+
+    @pl.when(core == 1)
+    def _():
+        z_copy(2).start()
 
     for j in range(SH):
         for d in range(1, NY):
@@ -424,7 +445,7 @@
     def p_copy(b, j, d):
         n = (b * 3 + j) * 3 + d - 1
         return remote(
-            product_out.at[pl.ds(n * B, B), :], product.at[rows_of(place(b, j)), :],
+            product_out.at[pl.ds(n * B, B), :], product_ref.at[rows_of(place(b, j)), :],
             p_send.at[n], p_recv.at[n], y_peer(d),
         )
 
@@ -433,8 +454,15 @@
         source = lax.rem(c + NY - d, NY)
         index = 3 * (2 * lax.rem(x + source + j, NX) + (zh if b == 0 else 1 - zh)) + j
         return remote(
-            product_out.at[pl.ds(n * B, B), :], product.at[rows_of(index), :],
+            product_out.at[pl.ds(n * B, B), :], product_ref.at[rows_of(index), :],
             p_send.at[n], p_recv.at[n], y_peer(NY - d),
+        )
+
+    def p_own(b, j):
+        n = 18 + b * 3 + j
+        return pltpu.make_async_copy(
+            product_out.at[pl.ds(n * B, B), :], product_ref.at[rows_of(place(b, j)), :],
+            p_local.at[b * 3 + j],
         )
 
     def times(a, b):
@@ -454,11 +482,11 @@
                     times(high, own_lo[span, :]) + times(low, own_hi[span, :])
                     + times(high, own_hi[span, :])
                 )
+                n = 18 + b * 3 + j if d == 0 else (b * 3 + j) * 3 + d - 1
+                product_out[n * B : (n + 1) * B, :] = got
                 if d == 0:
-                    product[rows_of(place(b, j)), :] = got
+                    p_own(b, j).start()
                 else:
-                    n = (b * 3 + j) * 3 + d - 1
-                    product_out[n * B : (n + 1) * B, :] = got
                     p_copy(b, j, d).start()
 
     panel_ref[...] = own[
@@ -471,39 +499,43 @@
 
     x_wait(2)
 
-    @pl.when(r > 0)
-    def _():
-        z_copy(0).wait_recv()
-
-    z_copy(1).wait_recv()
-    z_copy(2).wait_recv()
-
-    def put_front(i, j, value):
+    def sum_copy(part):
+        span = pl.ds(part * W, W)
+        return pltpu.make_async_copy(out_part.at[span, :], sum_ref.at[span, :], sum_sem.at[part])
+
+    def put_sum(i, j, value):
         span = (rows_of(i), slice(j * B, (j + 1) * B))
-        front_ref[span] = value + in_part[span]
-
-    spread(0, PB, 0, put_front)
+        out_part[span] = value + in_part[span]
+
+    for part in range(3):
+        z_copy(part).wait_send()
+        if part > 0:
+            z_copy(part).wait_recv()
+            spread(part * WT, (part + 1) * WT, 0, put_sum)
+        else:
+
+            @pl.when(r == 0)
+            def _():
+                out_part[0:W, :] = in_part[0:W, :]
+
+            @pl.when(r > 0)
+            def _():
+                z_copy(0).wait_recv()
+                spread(0, WT, 0, put_sum)
+
+        sum_copy(part).start()
 
     for b in range(2):
         for j in range(SH):
             for d in range(1, NY):
                 p_arrival(b, j, d).wait_recv()
-
-    @pl.loop(0, PB)
-    def _(i):
-        for j in range(SH):
-            down = r * PB + i - WT
-            right = c * PB + g * SH + j - WT
-            weight = pattern_ref[jnp.maximum(down, 0), jnp.maximum(right, 0)]
-            weight = jnp.where((down >= 0) & (right >= 0), weight, 0).astype(jnp.float32)
-            span = (rows_of(i), slice(j * B, (j + 1) * B))
-            front_ref[span] = front_ref[span] - weight * product[span]
+            p_own(b, j).wait()
+    for part in range(3):
+        sum_copy(part).wait()
 
     for k in range(4):
         for d in range(1, NX):
             x_copy(k, d).wait_send()
-    for part in range(3):
-        z_copy(part).wait_send()
 
     @pl.when(r > 0)
     def _():
@@ -534,57 +566,72 @@
                 p_copy(b, j, d).wait_send()
 
 
+def update_kernel(pattern_ref, sum_ref, product_ref, panel_in, front_ref, panel_ref):
+    step = pl.program_id(0)
+    r = lax.axis_index("row")
+    panel_ref[...] = panel_in[...]
+    for i in range(SH):
+        for j in range(SH):
+            down = r * PB + step * SH + i - WT
+            right = lax.axis_index("col") * PB + lax.axis_index("grp") * SH + j - WT
+            weight = pattern_ref[jnp.maximum(down, 0), jnp.maximum(right, 0)]
+            weight = jnp.where((down >= 0) & (right >= 0), weight, 0).astype(jnp.float32)
+            span = (slice(i * B, (i + 1) * B), slice(j * B, (j + 1) * B))
+            front_ref[span] = sum_ref[span] - weight * product_ref[span]
+
+
 def per_device(children, child_map, panel_inverse, pattern):
     anywhere = pl.BlockSpec(memory_space=pl.ANY)
     smem = pl.BlockSpec(memory_space=pltpu.SMEM)
     vmem = pl.BlockSpec(memory_space=pltpu.VMEM)
-    pack, rows, cols = pl.pallas_call(
-        pack_kernel,
-        name="pack",
-        out_shape=(
-            jax.ShapeDtypeStruct((2, GROUPS, SLOTS, B), jnp.float32),
-            jax.ShapeDtypeStruct((2 * NX * PB,), jnp.int32),
-            jax.ShapeDtypeStruct((2 * NX * 4,), jnp.int32),
-        ),
-        in_specs=[smem, anywhere],
-        out_specs=(anywhere, smem, smem),
-        scratch_shapes=[
-            pltpu.VMEM((CB * B, CB * B), jnp.float32),
-            pltpu.SemaphoreType.DMA((4,)),
-            pltpu.SemaphoreType.DMA((2, CB)),
-        ],
-        compiler_params=pltpu.CompilerParams(vmem_limit_bytes=60 * 2**20),
-    )(child_map, children[0])
-    pack = pack.reshape(2, GROUPS, TILES, B, B)
     f32, bf16 = jnp.float32, jnp.bfloat16
     dma = pltpu.SemaphoreType.DMA
     chunk = pltpu.VMEM((ZERO + 1, B, B), f32)
-    return pl.pallas_call(
+    sums, product, panel = pl.pallas_call(
         front_kernel,
         name="front",
         out_shape=(
             jax.ShapeDtypeStruct((BIG, WIDTH), f32),
+            jax.ShapeDtypeStruct((BIG, WIDTH), f32),
             jax.ShapeDtypeStruct((256, WIDTH), f32),
         ),
-        in_specs=[smem, smem, smem, anywhere, anywhere],
-        out_specs=(vmem, vmem),
+        in_specs=[smem, anywhere, anywhere],
+        out_specs=(anywhere, anywhere, vmem),
         scratch_shapes=[
+            pltpu.SMEM((2 * NX * PB,), jnp.int32), pltpu.SMEM((2 * NX * 4,), jnp.int32),
+            pltpu.VMEM((CB, HALF, B, B), f32), pltpu.VMEM((4, NX - 1, TILES, B, B), f32),
             chunk, chunk, chunk, chunk,
             pltpu.VMEM((BIG, WIDTH), f32), pltpu.VMEM((BIG, WIDTH), f32),
-            pltpu.VMEM((BIG, WIDTH), f32), pltpu.VMEM((18 * B, WIDTH), f32),
+            pltpu.VMEM((24 * B, WIDTH), f32),
             pltpu.VMEM((NY * WIDTH, W), f32),
             pltpu.VMEM((NY * WIDTH, W), bf16), pltpu.VMEM((NY * WIDTH, W), bf16),
             pltpu.VMEM((WIDTH, W), f32), pltpu.VMEM((WIDTH, W), f32),
             pltpu.VMEM((W, W), f32),
             pltpu.VMEM((W, WIDTH), bf16), pltpu.VMEM((W, WIDTH), bf16),
-            dma((12,)), dma((12,)), dma((4,)), dma((3,)), dma((3,)), dma(()), dma((3,)), dma(()),
-            dma((9,)), dma((3,)), dma((12,)), dma((12,)), dma((9,)), dma((9,)), dma((3,)), dma((3,)), dma((3,)), dma((3,)), dma((3,)),
-            dma((18,)), dma((18,)), pltpu.SemaphoreType.REGULAR,
+            dma((2, CB)), dma((12,)), dma((12,)), dma((3,)), dma((3,)), dma(()), dma((3,)), dma(()),
+            dma((9,)), dma((3,)), dma((12,)), dma((12,)), dma((9,)), dma((9,)),
+            dma((3,)), dma((3,)), dma((3,)), dma((3,)), dma((3,)),
+            dma((18,)), dma((18,)), dma((6,)), dma((3,)), pltpu.SemaphoreType.REGULAR,
         ],
         compiler_params=pltpu.CompilerParams(
-            collective_id=1, has_side_effects=True, vmem_limit_bytes=62 * 2**20
+            collective_id=1, has_side_effects=True, vmem_limit_bytes=63 * 2**20
         ),
-    )(rows, cols, pattern, pack, panel_inverse)
+    )(child_map, children.reshape(CB, B, CB * B), panel_inverse)
+    rows = SH * B
+    block = pl.BlockSpec((rows, WIDTH), lambda i: (i, 0))
+    part = pl.BlockSpec((256 // GROUPS, WIDTH), lambda i: (i, 0))
+    return pl.pallas_call(
+        update_kernel,
+        name="update",
+        grid=(BIG // rows,),
+        out_shape=(
+            jax.ShapeDtypeStruct((BIG, WIDTH), f32),
+            jax.ShapeDtypeStruct((256, WIDTH), f32),
+        ),
+        in_specs=[smem, block, block, part],
+        out_specs=(block, part),
+        compiler_params=pltpu.CompilerParams(vmem_limit_bytes=60 * 2**20),
+    )(pattern, sums, product, panel)
 
 
 def solution(mesh):

time: 224 us -> 212 us (0.946)
  local copies, waits for them, and re-layouts: 5.63 us -> 0 us
  Pallas kernels: 216 us -> 211 us
    unnamed x4 -> x0, local copies, waits for them, and re-layouts: 5.63 us -> none
    pallas_call x1, Pallas kernels: 208 us -> 202 us  [per_device(): pl.pallas_call(front_kernel, name='front', out_shape=(jax.ShapeDtypeStruc...]
where the time goes in v3:
time: 212 us; the launch traced here: 211 us
  Pallas kernels  211 us (100%)
    pallas_call x1, Pallas kernels, per_device(): pl.pallas_call(front_kernel, name='front', out_shape=(jax.ShapeDtypeStruc...  202 us
    pallas_call x1, Pallas kernels, per_device(): pl.pallas_call(update_kernel, name='update', grid=(BIG // rows,), out_sha...  8.4 us

profile of v3, /device:TPU:7, one launch (start us, length us, event | category | flops | bytes accessed | tf_op | source)
XLA Modules:
  0.0 211.2 jit_solution(5586725384572788436)
XLA Ops:
  0.6 202.2 %front.1 = (f32[3072,384]{1,0:T(8,128)}, f32[3072,384]{1,0:T(8,128)}, f32[256,384]{1,0:T(8,128)}) custom-call(s32[8,48]{1,0:T(8,128)} %map_ref.1, f32[12,128,1536]{2,1,0:T(8,128)} %bitcast.1, f32[256,1024]{1,0:T(8,128)} %inverse_ref.1), custom_call_target="tpu_custom_call" | custom-call | tf_op jit(solution)/shard_map/front/pallas_call | solution.py:590
  202.8 8.4 %update.1 = (f32[3072,384]{1,0:T(8,128)}, f32[256,384]{1,0:T(8,128)}) custom-call(s32[88,88]{1,0:T(8,128)} %pattern_ref.1, f32[3072,384]{1,0:T(8,128)} %get-tuple-element.5.sum_ref, f32[3072,384]{1,0:T(8,128)} %get-tuple-element.6.product_ref, f32[256,384]{1,0:T(8,128)} %get-tuple-element.7.panel_in), custom_call_target="tpu_custom_call" | custom-call | tf_op jit(solution)/shard_map/update/pallas_call | solution.py:623

commit v4 on v3

--- a/solution.py
+++ b/solution.py
@@ -1,5 +1,3 @@
-import functools
-
 import jax
 import jax.numpy as jnp
 from jax import lax
@@ -25,6 +23,7 @@
 NONE = 1000
 WIDTH = SH * B
 BIG = 3072
+STEPS = 2
 
 
 def front_kernel(
@@ -34,7 +33,7 @@
     as_ref, ao_ref, bs_ref, bo_ref,
     out_part, in_part, product_out,
     own, own_hi, own_lo, near, far,
-    inverse_all, top_hi, top_lo,
+    inverse_all,
     held_sem, x_send, x_recv, z_send, z_recv, i_send, i_recv, i_local,
     r_send, r_recv, c_send, c_recv, y_send, y_recv, n_send, n_recv, n_local, f_send, f_recv,
     p_send, p_recv, p_local, sum_sem, go,
@@ -253,21 +252,14 @@
         n = (d - 1) * 3 + j
         return remote(part, part, y_send.at[n], y_recv.at[n], y_peer(NY - d))
 
+    def times(a, b):
+        return lax.dot_general(a, b, (((1,), (1,)), ((), ())), preferred_element_type=jnp.float32)
+
     @pl.when(r == 0)
     def _():
         x_wait(1)
         spread(0, WT, 1, put_out)
         z_copy(0).start()
-        x_wait(0)
-        x_start(3)
-
-        z_copy(0).wait_recv()
-
-        def put_top(i, j, value):
-            span = (rows_of(i), slice(j * B, (j + 1) * B))
-            in_part[span] = in_part[span] + value
-
-        spread(0, WT, 0, put_top)
         for k in range(1, 4):
             remote(
                 inverse_ref, inverse_all.at[pl.ds(k * 256, 256), :],
@@ -277,18 +269,34 @@
 
         @pl.loop(0, WT)
         def _(i):
-            value = in_part[rows_of(i), :]
+            value = inverse_all[rows_of(i), :]
             high = value.astype(jnp.bfloat16)
-            top_hi[rows_of(i), :] = high
-            top_lo[rows_of(i), :] = (value - high.astype(jnp.float32)).astype(jnp.bfloat16)
-
+            own_hi[rows_of(i), :] = high
+            own_lo[rows_of(i), :] = (value - high.astype(jnp.float32)).astype(jnp.bfloat16)
+
+        x_wait(0)
+        x_start(3)
+
+        z_copy(0).wait_recv()
+
+        def put_top(i, j, value):
+            span = (rows_of(i), slice(j * B, (j + 1) * B))
+            in_part[span] = in_part[span] + value
+
+        spread(0, WT, 0, put_top)
+        top = slice(W, W + WIDTH)
+        for i in range(WT):
+            value = in_part[i * B : (i + 1) * B, :].T
+            high = value.astype(jnp.bfloat16)
+            own_hi[top, i * B : (i + 1) * B] = high
+            own_lo[top, i * B : (i + 1) * B] = (value - high.astype(jnp.float32)).astype(jnp.bfloat16)
         for k in range(4):
-            block = inverse_all[k * 256 : (k + 1) * 256, :]
-            high = block.astype(jnp.bfloat16)
-            low = (block - high.astype(jnp.float32)).astype(jnp.bfloat16)
-            dot = functools.partial(jnp.dot, preferred_element_type=jnp.float32)
-            part = dot(high, top_lo[...]) + dot(low, top_hi[...]) + dot(high, top_hi[...])
-            own[pl.ds(pl.multiple_of(c * WIDTH, WIDTH), WIDTH), k * 256 : (k + 1) * 256] = part.T
+            part = slice(k * 256, (k + 1) * 256)
+            own[pl.ds(pl.multiple_of(c * WIDTH, WIDTH), WIDTH), part] = (
+                times(own_hi[top, :], own_lo[part, :])
+                + times(own_lo[top, :], own_hi[part, :])
+                + times(own_hi[top, :], own_hi[part, :])
+            )
         for j in range(SH):
             r_copy(j, 2).start()
             r_copy(j, 3).start()
@@ -343,9 +351,7 @@
 
     spread(WT, PB, 1, put_out)
 
-    @pl.when(r != 1)
-    def _():
-        z_copy(1).start()
+    z_copy(1).start()
 
     @pl.when(core == 0)
     def _():
@@ -416,10 +422,6 @@
             n_own(j).wait()
 
         f_copy(j).start()
-
-    @pl.when(r == 1)
-    def _():
-        z_copy(1).start()
 
     @pl.when(core == 1)
     def _():
@@ -464,9 +466,6 @@
             product_out.at[pl.ds(n * B, B), :], product_ref.at[rows_of(place(b, j)), :],
             p_local.at[b * 3 + j],
         )
-
-    def times(a, b):
-        return lax.dot_general(a, b, (((1,), (1,)), ((), ())), preferred_element_type=jnp.float32)
 
     for b in range(2):
         for j in range(SH):
@@ -497,8 +496,6 @@
     def _():
         x_wait(0)
 
-    x_wait(2)
-
     def sum_copy(part):
         span = pl.ds(part * W, W)
         return pltpu.make_async_copy(out_part.at[span, :], sum_ref.at[span, :], sum_sem.at[part])
@@ -524,6 +521,8 @@
                 spread(0, WT, 0, put_sum)
 
         sum_copy(part).start()
+        if part == 0:
+            x_wait(2)
 
     for b in range(2):
         for j in range(SH):
@@ -570,9 +569,9 @@
     step = pl.program_id(0)
     r = lax.axis_index("row")
     panel_ref[...] = panel_in[...]
-    for i in range(SH):
+    for i in range(PB // STEPS):
         for j in range(SH):
-            down = r * PB + step * SH + i - WT
+            down = r * PB + step * (PB // STEPS) + i - WT
             right = lax.axis_index("col") * PB + lax.axis_index("grp") * SH + j - WT
             weight = pattern_ref[jnp.maximum(down, 0), jnp.maximum(right, 0)]
             weight = jnp.where((down >= 0) & (right >= 0), weight, 0).astype(jnp.float32)
@@ -607,7 +606,6 @@
             pltpu.VMEM((NY * WIDTH, W), bf16), pltpu.VMEM((NY * WIDTH, W), bf16),
             pltpu.VMEM((WIDTH, W), f32), pltpu.VMEM((WIDTH, W), f32),
             pltpu.VMEM((W, W), f32),
-            pltpu.VMEM((W, WIDTH), bf16), pltpu.VMEM((W, WIDTH), bf16),
             dma((2, CB)), dma((12,)), dma((12,)), dma((3,)), dma((3,)), dma(()), dma((3,)), dma(()),
             dma((9,)), dma((3,)), dma((12,)), dma((12,)), dma((9,)), dma((9,)),
             dma((3,)), dma((3,)), dma((3,)), dma((3,)), dma((3,)),
@@ -617,13 +615,12 @@
             collective_id=1, has_side_effects=True, vmem_limit_bytes=63 * 2**20
         ),
     )(child_map, children.reshape(CB, B, CB * B), panel_inverse)
-    rows = SH * B
-    block = pl.BlockSpec((rows, WIDTH), lambda i: (i, 0))
-    part = pl.BlockSpec((256 // GROUPS, WIDTH), lambda i: (i, 0))
+    block = pl.BlockSpec((BIG // STEPS, WIDTH), lambda i: (i, 0))
+    part = pl.BlockSpec((256 // STEPS, WIDTH), lambda i: (i, 0))
     return pl.pallas_call(
         update_kernel,
         name="update",
-        grid=(BIG // rows,),
+        grid=(STEPS,),
         out_shape=(
             jax.ShapeDtypeStruct((BIG, WIDTH), f32),
             jax.ShapeDtypeStruct((256, WIDTH), f32),

time: 212 us -> 200 us (0.943); the launches traced: 211 us -> 197 us
  Pallas kernels: 211 us -> 196 us
    pallas_call x1, Pallas kernels: 202 us -> 190 us  [per_device(): pl.pallas_call(front_kernel, name='front', out_shape=(jax.ShapeDtypeStruc...]
    pallas_call x1, Pallas kernels: 8.4 us -> 6.05 us  [per_device(): pl.pallas_call(update_kernel, name='update', grid=(STEPS,), out_shape=(ja...]
where the time goes in v4:
time: 200 us; the launch traced here: 197 us
  Pallas kernels  196 us (98%)
    pallas_call x1, Pallas kernels, per_device(): pl.pallas_call(front_kernel, name='front', out_shape=(jax.ShapeDtypeStruc...  190 us
    pallas_call x1, Pallas kernels, per_device(): pl.pallas_call(update_kernel, name='update', grid=(STEPS,), out_shape=(ja...  6.05 us

profile of v4, /device:TPU:7, one launch (start us, length us, event | category | flops | bytes accessed | tf_op | source)
XLA Modules:
  0.0 196.9 jit_solution(11036772221022424438)
XLA Ops:
  0.6 190.3 %front.1 = (f32[3072,384]{1,0:T(8,128)}, f32[3072,384]{1,0:T(8,128)}, f32[256,384]{1,0:T(8,128)}) custom-call(s32[8,48]{1,0:T(8,128)} %map_ref.1, f32[12,128,1536]{2,1,0:T(8,128)} %bitcast.1, f32[256,1024]{1,0:T(8,128)} %inverse_ref.1), custom_call_target="tpu_custom_call" | custom-call | tf_op jit(solution)/shard_map/front/pallas_call | solution.py:589
  190.9 6.0 %update.1 = (f32[3072,384]{1,0:T(8,128)}, f32[256,384]{1,0:T(8,128)}) custom-call(s32[88,88]{1,0:T(8,128)} %pattern_ref.1, f32[3072,384]{1,0:T(8,128)} %get-tuple-element.5.sum_ref, f32[3072,384]{1,0:T(8,128)} %get-tuple-element.6.product_ref, f32[256,384]{1,0:T(8,128)} %get-tuple-element.7.panel_in), custom_call_target="tpu_custom_call" | custom-call | tf_op jit(solution)/shard_map/update/pallas_call | solution.py:620

commit v5 on v4

--- a/solution.py
+++ b/solution.py
@@ -290,14 +290,16 @@
             high = value.astype(jnp.bfloat16)
             own_hi[top, i * B : (i + 1) * B] = high
             own_lo[top, i * B : (i + 1) * B] = (value - high.astype(jnp.float32)).astype(jnp.bfloat16)
-        for k in range(4):
-            part = slice(k * 256, (k + 1) * 256)
-            own[pl.ds(pl.multiple_of(c * WIDTH, WIDTH), WIDTH), part] = (
-                times(own_hi[top, :], own_lo[part, :])
-                + times(own_lo[top, :], own_hi[part, :])
-                + times(own_hi[top, :], own_hi[part, :])
-            )
         for j in range(SH):
+            piece = slice(W + j * B, W + (j + 1) * B)
+            rows = pl.ds(pl.multiple_of(c * WIDTH + j * B, B), B)
+            for k in range(4):
+                part = slice(k * 256, (k + 1) * 256)
+                own[rows, part] = (
+                    times(own_hi[piece, :], own_lo[part, :])
+                    + times(own_lo[piece, :], own_hi[part, :])
+                    + times(own_hi[piece, :], own_hi[part, :])
+                )
             r_copy(j, 2).start()
             r_copy(j, 3).start()
             r_copy(j, 1).start()

time: 200 us -> 199 us (level)
  no operation moved by 1% of the time
where the time goes in v5:
time: 199 us; the launch traced here: 196 us
  Pallas kernels  196 us (98%)
    pallas_call x1, Pallas kernels, per_device(): pl.pallas_call(front_kernel, name='front', out_shape=(jax.ShapeDtypeStruc...  190 us
    pallas_call x1, Pallas kernels, per_device(): pl.pallas_call(update_kernel, name='update', grid=(STEPS,), out_shape=(ja...  6.05 us

profile of v5, /device:TPU:7, one launch (start us, length us, event | category | flops | bytes accessed | tf_op | source)
XLA Modules:
  0.0 196.4 jit_solution(15561737883727031072)
XLA Ops:
  0.6 189.7 %front.1 = (f32[3072,384]{1,0:T(8,128)}, f32[3072,384]{1,0:T(8,128)}, f32[256,384]{1,0:T(8,128)}) custom-call(s32[8,48]{1,0:T(8,128)} %map_ref.1, f32[12,128,1536]{2,1,0:T(8,128)} %bitcast.1, f32[256,1024]{1,0:T(8,128)} %inverse_ref.1), custom_call_target="tpu_custom_call" | custom-call | tf_op jit(solution)/shard_map/front/pallas_call | solution.py:591
  190.4 6.0 %update.1 = (f32[3072,384]{1,0:T(8,128)}, f32[256,384]{1,0:T(8,128)}) custom-call(s32[88,88]{1,0:T(8,128)} %pattern_ref.1, f32[3072,384]{1,0:T(8,128)} %get-tuple-element.5.sum_ref, f32[3072,384]{1,0:T(8,128)} %get-tuple-element.6.product_ref, f32[256,384]{1,0:T(8,128)} %get-tuple-element.7.panel_in), custom_call_target="tpu_custom_call" | custom-call | tf_op jit(solution)/shard_map/update/pallas_call | solution.py:622
